TPU v7x, 256 devices: a whole 4x4x8 slice. The times are simulated.
256 devices in a mesh: segment: 2 (over y_hi), shard: 64 (over x, y_lo, z), chan: 2 (over core).
Axes of the slice: x: 4, y: 4 (y_hi: 2, y_lo: 2; y = y_hi * 2 + y_lo), z: 8, core: 2. Of those that a mesh axis runs over, the one named last changes fastest.
Arguments:
- echoes: bfloat16 [2, 8192, 16384], P(None, ('chan', 'segment', 'shard')), parts along dimension 1, may hold values from -6 to 6
- replica: float32 [2, 2048], replicated, may hold values from -0.09375 to 0.09375
- rcmc_weights: float32 [8, 4096], replicated, may hold values from -2 to 2
- az_filter: bfloat16 [2, 4096, 16384], P(None, None, ('segment', 'shard')), may hold values from -4.1875 to 4.1875
Outputs:
- image: float32 [2, 8192, 16384], P(None, 'chan', ('segment', 'shard')), parts along dimension 1
There are 2 independent parts, one for each index of `chan`. A program takes and returns all parts, laid end to end along the dimension named above; an argument that names none is the same for every part. Nothing has to cross between parts.
All inputs are finite; a program needn't handle non-finite values.
Results may differ from a plain program's by a relative error of at most 0.0003.
Values sent between devices are 32-bit elements; how exact they have to be, the bound alone decides.
A program may use at most 128 MiB of HBM per device.

v0:
```python
import functools
import math

import jax
import jax.numpy as jnp
import ml_dtypes
import numpy as np
from jax import lax
from jax.experimental import pallas as pl
from jax.experimental.pallas import tpu as pltpu
from jax.sharding import PartitionSpec as P

MESH = pl.DeviceIdType.MESH
F32 = jnp.float32
BF16 = jnp.bfloat16
TAPS = 8
HALF = TAPS // 2
N = 128
J = 32
CHUNKS = ((0, 4), (4, 8), (12, 8), (20, 12))


def constant_tables():
    k = np.arange(N)
    ang = 2.0 * np.pi * ((k[:, None] * k[None, :]) % N) / N
    c, s = np.cos(ang), -np.sin(ang)
    left = np.block([[c, -s], [s, c]]).astype(np.float32)
    mats = []
    for m in (left, left.T):
        hi = m.astype(ml_dtypes.bfloat16)
        lo = (m - hi.astype(np.float32)).astype(ml_dtypes.bfloat16)
        mats += [hi, lo]
    mats = np.stack(mats)
    ang = 2.0 * np.pi * (k[:, None] * k[None, :]) / (N * N)
    twist = np.stack([np.cos(ang), -np.sin(ang)]).astype(np.float32)
    j = np.arange(J)
    ang = 2.0 * np.pi * (j[:, None] * k[None, :]) / (N * J)
    az = np.stack([np.cos(ang), -np.sin(ang)], axis=1).astype(np.float32)
    az = np.ascontiguousarray(np.broadcast_to(az[..., None], (J, 2, N, N)))
    return mats, twist, az


def split(v):
    hi = v.astype(BF16)
    return hi, (v - hi.astype(F32)).astype(BF16)


def dot(a, b):
    return jnp.dot(a, b, preferred_element_type=F32)


def left_mul(hi, lo, data):
    d_hi, d_lo = split(data)
    return dot(hi, d_hi) + dot(lo, d_hi) + dot(hi, d_lo)


def right_mul(data, hi, lo):
    d_hi, d_lo = split(data)
    return dot(d_hi, hi) + dot(d_lo, hi) + dot(d_hi, lo)


def add(a, b):
    return (a[0] + b[0], a[1] + b[1])


def sub(a, b):
    return (a[0] - b[0], a[1] - b[1])


def turn(a, angle_num, angle_den, sign):
    q = (8 * angle_num) % (8 * angle_den)
    if q == 0:
        return a
    if q == 2 * angle_den:
        return (-a[1], a[0]) if sign > 0 else (a[1], -a[0])
    if q == 4 * angle_den:
        return (-a[0], -a[1])
    if q == 6 * angle_den:
        return (a[1], -a[0]) if sign > 0 else (-a[1], a[0])
    ang = sign * 2.0 * math.pi * angle_num / angle_den
    c, s = math.cos(ang), math.sin(ang)
    return (a[0] * c - a[1] * s, a[0] * s + a[1] * c)


def fft(xs, sign):
    n = len(xs)
    if n == 1:
        return xs
    even, odd = fft(xs[0::2], sign), fft(xs[1::2], sign)
    out = [None] * n
    for k in range(n // 2):
        t = turn(odd[k], k, n, sign)
        out[k] = add(even[k], t)
        out[k + n // 2] = sub(even[k], t)
    return out


def fft32(xs, sign):
    cols = []
    for low in range(4):
        col = fft([xs[4 * high + low] for high in range(8)], sign)
        cols.append([turn(col[k], low * k, 32, sign) for k in range(8)])
    out = [None] * 32
    for k in range(8):
        four = fft([cols[low][k] for low in range(4)], sign)
        for k0 in range(4):
            out[k + 8 * k0] = four[k0]
    return out


def body(
    echoes, replica, weights, az_filter, mats_h, twist_h, aztw_h, out,
    e_v, u_v, rep_v, x_v, kern_v, s_v, r_v, y_v, w_t, w_b, azf_v, az_v, mats, twist, aztw,
    p_r, p_l, h_l, h_r, o_v, in_sem, send_sem, recv_sem, own_sem, halo_send, halo_recv, out_sem,
):
    seg, sh = lax.axis_index("segment"), lax.axis_index("shard")
    x, y, z = sh // 16, seg * 2 + (sh // 8) % 2, sh % 8
    me = seg * 64 + sh

    def peer(i):
        px, py, pz = (x + i // 32) % 4, (y + (i // 8) % 4) % 4, (z + i % 8) % 8
        s, h = py // 2, (px * 2 + py % 2) * 8 + pz
        return s, h, s * 64 + h

    loads = [
        pltpu.make_async_copy(replica, rep_v, in_sem.at[0]),
        pltpu.make_async_copy(mats_h, mats, in_sem.at[1]),
        pltpu.make_async_copy(twist_h, twist, in_sem.at[2]),
        pltpu.make_async_copy(echoes.at[:, pl.ds(0, 16)], e_v.at[:, pl.ds(0, 16)], in_sem.at[3]),
        pltpu.make_async_copy(echoes.at[:, pl.ds(16, 16)], e_v.at[:, pl.ds(16, 16)], in_sem.at[4]),
        pltpu.make_async_copy(weights, w_t, in_sem.at[5]),
        pltpu.make_async_copy(az_filter, az_v, in_sem.at[6]),
        pltpu.make_async_copy(aztw_h, aztw, in_sem.at[7]),
    ]
    for load in loads:
        load.start()
    barrier = pltpu.get_barrier_semaphore()

    def greet(i, c):
        s, h, _ = peer(i)
        pl.semaphore_signal(
            barrier, inc=1, device_id={"segment": s, "shard": h}, device_id_type=MESH
        )
        return c

    lax.fori_loop(1, N, greet, 0)

    for i in range(3):
        loads[i].wait()
    x_v[...] = jnp.zeros_like(x_v)
    for a in range(16):
        x_v[pl.ds(a, 1), :] = rep_v[0:1, 128 * a : 128 * a + 128]
        x_v[pl.ds(128 + a, 1), :] = rep_v[1:2, 128 * a : 128 * a + 128]
    t_re, t_im = twist[0], twist[1]
    mid = left_mul(mats[0], mats[1], x_v[...])
    m_re, m_im = mid[:N], mid[N:]
    mid = jnp.concatenate([m_re * t_re - m_im * t_im, m_re * t_im + m_im * t_re], axis=1)
    spec = right_mul(mid, mats[2], mats[3]) * (1.0 / (N * N))
    kern_v[0] = spec[:, :N]
    kern_v[1] = spec[:, N:]

    def unpack(half):
        def one(a, c):
            cols = pl.ds(pl.multiple_of(a * 128, 128), 128)
            rows = pl.ds(pl.multiple_of(a * 16, 16), 16)
            for part in range(2):
                u_v[part, rows, :] = e_v[part, pl.ds(16 * half, 16), cols].astype(F32)
            return c

        lax.fori_loop(0, N, one, 0, unroll=8)

    def compress(pair, c):
        p = (2 * pair) % 16
        data = jnp.concatenate(
            [
                jnp.concatenate(
                    [u_v[part, pl.ds(p + i, N, stride=16), :] for part in range(2)], axis=0
                )
                for i in range(2)
            ],
            axis=1,
        ).astype(BF16)
        mid = dot(mats[0], data) + dot(mats[1], data)
        rows = []
        for i in range(2):
            m_re, m_im = mid[:N, i * N : i * N + N], mid[N:, i * N : i * N + N]
            rows.append(
                jnp.concatenate(
                    [m_re * twist[0] - m_im * twist[1], m_re * twist[1] + m_im * twist[0]], axis=1
                )
            )
        spec = right_mul(jnp.concatenate(rows, axis=0), mats[2], mats[3])
        rows = []
        for i in range(2):
            s_re, s_im = spec[i * N : i * N + N, :N], spec[i * N : i * N + N, N:]
            rows.append(
                jnp.concatenate(
                    [s_re * kern_v[0] + s_im * kern_v[1], s_im * kern_v[0] - s_re * kern_v[1]],
                    axis=1,
                )
            )
        mid = right_mul(jnp.concatenate(rows, axis=0), mats[0], mats[1])
        cols = []
        for i in range(2):
            m_re, m_im = mid[i * N : i * N + N, :N], mid[i * N : i * N + N, N:]
            cols.append(
                jnp.concatenate(
                    [m_re * twist[0] + m_im * twist[1], m_im * twist[0] - m_re * twist[1]], axis=0
                )
            )
        done = left_mul(mats[2], mats[3], jnp.concatenate(cols, axis=1))
        for i in range(2):
            for part in range(2):
                s_v[2 * pair + i, part] = done[part * N : part * N + N, i * N : i * N + N]
        return c

    def send(n):
        first, count = CHUNKS[n]
        rows = pl.ds(first, count)
        pltpu.make_async_copy(s_v.at[rows, :, me], r_v.at[rows, :, me], own_sem.at[n]).start()

        def one(i, c):
            s, h, at = peer(i)
            pltpu.make_async_remote_copy(
                src_ref=s_v.at[rows, :, at],
                dst_ref=r_v.at[rows, :, me],
                send_sem=send_sem.at[n],
                recv_sem=recv_sem.at[n],
                device_id={"segment": s, "shard": h},
                device_id_type=MESH,
            ).start()
            return c

        lax.fori_loop(1, N, one, 0)

    loads[3].wait()
    unpack(0)
    half = 0
    for n, (first, count) in enumerate(CHUNKS):
        start = first
        if first < 16 < first + count:
            lax.fori_loop(first // 2, 8, compress, 0)
            start = 16
        if start >= 16 and half == 0:
            half = 1
            loads[4].wait()
            unpack(1)
        lax.fori_loop(start // 2, (first + count) // 2, compress, 0)
        if n == 0:
            pl.semaphore_wait(barrier, N - 1)
        send(n)

    loads[5].wait()

    def spread(g, c):
        cols = pl.ds(pl.multiple_of(g * 128, 128), 128)
        across = jnp.transpose(w_t[:, cols])
        for t in range(TAPS):
            w_b[t, cols, :] = jnp.broadcast_to(across[:, t : t + 1], (N, N))
        return c

    lax.fori_loop(0, J, spread, 0)
    loads[6].wait()

    def widen(g, c):
        rows = pl.ds(pl.multiple_of(g * 128, 128), 128)
        for part in range(2):
            azf_v[part, rows, :] = az_v[part, rows, :].astype(F32)
        return c

    lax.fori_loop(0, J, widen, 0)
    loads[7].wait()

    def over_devices(pair, c):
        data = jnp.concatenate(
            [
                jnp.concatenate([r_v[2 * pair + i, 0], r_v[2 * pair + i, 1]], axis=0)
                for i in range(2)
            ],
            axis=1,
        )
        mid = left_mul(mats[0], mats[1], data)
        for i in range(2):
            m_re, m_im = mid[:N, i * N : i * N + N], mid[N:, i * N : i * N + N]
            a_re, a_im = aztw[2 * pair + i, 0], aztw[2 * pair + i, 1]
            y_v[2 * pair + i, 0] = m_re * a_re - m_im * a_im
            y_v[2 * pair + i, 1] = m_re * a_im + m_im * a_re
        return c

    for n, (first, count) in enumerate(CHUNKS):
        rows = pl.ds(first, count)
        pltpu.make_async_copy(s_v.at[rows, :, me], r_v.at[rows, :, me], own_sem.at[n]).wait()
        landed = r_v.at[rows, :, pl.ds(0, N - 1)]
        pltpu.make_async_copy(landed, landed, recv_sem.at[n]).wait()
        lax.fori_loop(first // 2, (first + count) // 2, over_devices, 0)

    lane = lax.broadcasted_iota(jnp.int32, (8, N), 1)
    slot = lane % 8

    def over_pulses(blk, c):
        rows = pl.ds(pl.multiple_of(blk * 8, 8), 8)
        vals = fft32([(y_v[j, 0, rows, :], y_v[j, 1, rows, :]) for j in range(J)], -1)
        for f2 in range(J):
            y_v[f2, 0, rows, :] = vals[f2][0]
            y_v[f2, 1, rows, :] = vals[f2][1]
        for grp in range(2):
            packed = []
            for part in range(2):
                acc = jnp.zeros((8, N), F32)
                for g in range(16):
                    moved = pltpu.roll(vals[16 * grp + g][part], (8 * g + 4) % N, 1)
                    acc = jnp.where(lane // 8 == g, moved, acc)
                packed.append(acc)
            p_r[blk, grp] = jnp.where(slot < 4, packed[0], pltpu.roll(packed[1], 4, 1))
            p_l[blk, grp] = jnp.where(slot < 4, pltpu.roll(packed[0], N - 4, 1), packed[1])
        return c

    lax.fori_loop(0, 16, over_pulses, 0)
    after, before = (me + 1) % N, (me + N - 1) % N
    right = {"segment": after // 64, "shard": after % 64}
    left = {"segment": before // 64, "shard": before % 64}
    to_right = pltpu.make_async_remote_copy(
        src_ref=p_r, dst_ref=h_l, send_sem=halo_send.at[0], recv_sem=halo_recv.at[0],
        device_id=right, device_id_type=MESH,
    )
    to_left = pltpu.make_async_remote_copy(
        src_ref=p_l, dst_ref=h_r, send_sem=halo_send.at[1], recv_sem=halo_recv.at[1],
        device_id=left, device_id_type=MESH,
    )
    to_right.start()
    to_left.start()
    to_right.wait()
    to_left.wait()

    has_left = jnp.where(me == 0, 0.0, 1.0)
    has_right = jnp.where(me == N - 1, 0.0, 1.0)

    def focus(blk, c):
        rows = pl.ds(pl.multiple_of(blk * 8, 8), 8)
        halos = []
        for grp in range(2):
            lft = h_l[blk, grp] * has_left
            rgt = h_r[blk, grp] * has_right
            halos.append(
                (
                    jnp.where(slot < 4, lft, pltpu.roll(rgt, 4, 1)),
                    jnp.where(slot < 4, pltpu.roll(lft, N - 4, 1), rgt),
                )
            )
        vals = []
        for f2 in range(J):
            frows = pl.ds(pl.multiple_of(f2 * 128 + blk * 8, 8), 8)
            taps = [w_b[t, frows, :] for t in range(TAPS)]
            moved = []
            for part in range(2):
                own = y_v[f2, part, rows, :]
                edge = pltpu.roll(halos[f2 // 16][part], (N - 8 * (f2 % 16) - 4) % N, 1)
                acc = taps[HALF] * own
                for t in range(TAPS):
                    if t != HALF:
                        wrapped = lane < t - HALF if t > HALF else lane >= N - HALF + t
                        src = jnp.where(wrapped, edge, own)
                        acc = acc + taps[t] * pltpu.roll(src, (HALF - t) % N, 1)
                moved.append(acc)
            a_re, a_im = azf_v[0, frows, :], azf_v[1, frows, :]
            vals.append(
                (moved[0] * a_re - moved[1] * a_im, moved[0] * a_im + moved[1] * a_re)
            )
        vals = fft32(vals, 1)
        for j in range(J):
            a_re, a_im = aztw[j, 0, rows, :], aztw[j, 1, rows, :]
            v_re, v_im = vals[j]
            y_v[j, 0, rows, :] = v_re * a_re + v_im * a_im
            y_v[j, 1, rows, :] = v_im * a_re - v_re * a_im
        return c

    lax.fori_loop(0, 16, focus, 0)

    def finish(pair, c):
        data = jnp.concatenate(
            [
                jnp.concatenate([y_v[2 * pair + i, 0], y_v[2 * pair + i, 1]], axis=0)
                for i in range(2)
            ],
            axis=1,
        )
        done = left_mul(mats[2], mats[3], data) * (1.0 / (N * J))
        for i in range(2):
            for part in range(2):
                o_v[2 * pair + i, part] = done[part * N : part * N + N, i * N : i * N + N]
        for i in range(2):
            for part in range(2):
                pltpu.make_async_copy(
                    o_v.at[2 * pair + i, part], out.at[part, :, 2 * pair + i], out_sem
                ).start()
        return c

    lax.fori_loop(0, J // 2, finish, 0)
    pltpu.make_async_copy(o_v, o_v, out_sem).wait()
    for n, (first, count) in enumerate(CHUNKS):
        left_here = s_v.at[pl.ds(first, count), :, pl.ds(0, N - 1)]
        pltpu.make_async_copy(left_here, left_here, send_sem.at[n]).wait()


def shards(echoes, replica, rcmc_weights, az_filter):
    mats, twist, aztw = (jnp.asarray(t) for t in constant_tables())
    parts = len(CHUNKS)
    dma = pltpu.SemaphoreType.DMA
    out = pl.pallas_call(
        body,
        out_shape=jax.ShapeDtypeStruct((2, N, J, N), F32),
        in_specs=[pl.BlockSpec(memory_space=pl.ANY)] * 7,
        out_specs=pl.BlockSpec(memory_space=pl.ANY),
        scratch_shapes=[
            pltpu.VMEM((2, J, N * N), BF16),
            pltpu.VMEM((2, N * 16, N), F32),
            pltpu.VMEM((2, 2048), F32),
            pltpu.VMEM((2 * N, N), F32),
            pltpu.VMEM((2, N, N), F32),
            pltpu.VMEM((J, 2, N, N), F32),
            pltpu.VMEM((J, 2, N, N), F32),
            pltpu.VMEM((J, 2, N, N), F32),
            pltpu.VMEM((TAPS, N * J), F32),
            pltpu.VMEM((TAPS, N * J, N), F32),
            pltpu.VMEM((2, N * J, N), F32),
            pltpu.VMEM((2, N * J, N), BF16),
            pltpu.VMEM((4, 2 * N, 2 * N), BF16),
            pltpu.VMEM((2, N, N), F32),
            pltpu.VMEM((J, 2, N, N), F32),
            pltpu.VMEM((16, 2, 8, N), F32),
            pltpu.VMEM((16, 2, 8, N), F32),
            pltpu.VMEM((16, 2, 8, N), F32),
            pltpu.VMEM((16, 2, 8, N), F32),
            pltpu.VMEM((J, 2, N, N), F32),
            dma((8,)),
            dma((parts,)),
            dma((parts,)),
            dma((parts,)),
            dma((2,)),
            dma((2,)),
            dma(()),
        ],
        compiler_params=pltpu.CompilerParams(
            collective_id=0, has_side_effects=True, vmem_limit_bytes=60 * 2**20
        ),
        name="focus",
    )(echoes, replica, rcmc_weights, az_filter, mats, twist, aztw)
    return out.reshape(2, N * J, N)


def solution(mesh):
    return jax.shard_map(
        shards,
        mesh=mesh,
        in_specs=(
            P(None, ("chan", "segment", "shard"), None),
            P(),
            P(),
            P(None, None, ("segment", "shard")),
        ),
        out_specs=P(None, "chan", ("segment", "shard")),
        check_vma=False,
    )
```

profile of v0, /device:TPU:1, one launch (start us, length us, event | category | flops | bytes accessed | tf_op | source)
XLA Modules:
  0.0 184.5 jit_solution(9646629745467936820)
XLA Ops:
  0.0 180.1 %focus.1 = f32[2,128,32,128]{3,2,1,0:T(8,128)} custom-call(bf16[2,32,16384]{2,1,0:T(8,128)(2,1)} %echoes.1, f32[2,2048]{1,0:T(2,128)} %replica.1, f32[8,4096]{1,0:T(8,128)} %weights.1, bf16[2,4096,128]{2,1,0:T(8,128)(2,1)} %az_filter.1, bf16[4,256,256]{2,1,0:T(8,128)(2,1)} %constant.6.clone.mats_h, f32[2,128,128]{2,1,0:T(8,128)} %constant.7.clone.twist_h, ...), custom_call_target="tpu_custom_call" | custom-call | tf_op jit(solution)/shard_map/focus/pallas_call | solution.py:409
  180.1 4.5 %copy.9 = f32[2,4096,128]{2,1,0:T(8,128)} copy(f32[2,4096,128]{2,1,0:T(8,128)} %bitcast.1) | data formatting | bytes 8388608
where the time goes:
time: 185 us
  Pallas kernels  180 us (97%)
  local copies, waits for them, and re-layouts  4.47 us (2%)
    pallas_call x1, Pallas kernels, shards(): pl.pallas_call(body, out_shape=jax.ShapeDtypeStruct((2, N, J, N), F32), i...  180 us
    unnamed x1, local copies, waits for them, and re-layouts  4.47 us

commit v1 on v0

--- a/solution.py
+++ b/solution.py
@@ -37,7 +37,13 @@
     ang = 2.0 * np.pi * (j[:, None] * k[None, :]) / (N * J)
     az = np.stack([np.cos(ang), -np.sin(ang)], axis=1).astype(np.float32)
     az = np.ascontiguousarray(np.broadcast_to(az[..., None], (J, 2, N, N)))
-    return mats, twist, az
+    lanes = np.arange(N)
+    packed = np.where(lanes % 8 < HALF, lanes % 8 - HALF, N + lanes % 8 - HALF)
+    want = [lanes[None, :] + t - HALF for t in range(TAPS) if t != HALF]
+    own = np.concatenate([lanes[:, None] == w for w in want], axis=1)
+    edge = np.concatenate([packed[:, None] == w for w in want], axis=1)
+    shift = np.stack([np.tile(own, (2, 1)), np.tile(edge, (2, 1))]).astype(ml_dtypes.bfloat16)
+    return mats, twist, az, shift
 
 
 def split(v):
@@ -109,9 +115,9 @@
 
 
 def body(
-    echoes, replica, weights, az_filter, mats_h, twist_h, aztw_h, out,
-    e_v, u_v, rep_v, x_v, kern_v, s_v, r_v, y_v, w_t, w_b, azf_v, az_v, mats, twist, aztw,
-    p_r, p_l, h_l, h_r, o_v, in_sem, send_sem, recv_sem, own_sem, halo_send, halo_recv, out_sem,
+    echoes, replica, weights, az_filter, mats_h, twist_h, aztw_h, shift_h, out,
+    e_v, u_v, rep_v, x_v, kern_v, s_v, r_v, y_v, w_t, w_b, azf_v, az_v, mats, twist, aztw, shift,
+    p_r, p_l, h_l, h_r, h_c, in_sem, send_sem, recv_sem, own_sem, halo_send, halo_recv, out_sem,
 ):
     seg, sh = lax.axis_index("segment"), lax.axis_index("shard")
     x, y, z = sh // 16, seg * 2 + (sh // 8) % 2, sh % 8
@@ -131,6 +137,7 @@
         pltpu.make_async_copy(weights, w_t, in_sem.at[5]),
         pltpu.make_async_copy(az_filter, az_v, in_sem.at[6]),
         pltpu.make_async_copy(aztw_h, aztw, in_sem.at[7]),
+        pltpu.make_async_copy(shift_h, shift, in_sem.at[8]),
     ]
     for load in loads:
         load.start()
@@ -270,6 +277,7 @@
 
     lax.fori_loop(0, J, widen, 0)
     loads[7].wait()
+    loads[8].wait()
 
     def over_devices(pair, c):
         data = jnp.concatenate(
@@ -335,48 +343,66 @@
     has_left = jnp.where(me == 0, 0.0, 1.0)
     has_right = jnp.where(me == N - 1, 0.0, 1.0)
 
-    def focus(blk, c):
-        rows = pl.ds(pl.multiple_of(blk * 8, 8), 8)
-        halos = []
+    for blk in range(16):
         for grp in range(2):
             lft = h_l[blk, grp] * has_left
             rgt = h_r[blk, grp] * has_right
-            halos.append(
-                (
-                    jnp.where(slot < 4, lft, pltpu.roll(rgt, 4, 1)),
-                    jnp.where(slot < 4, pltpu.roll(lft, N - 4, 1), rgt),
-                )
-            )
-        vals = []
-        for f2 in range(J):
-            frows = pl.ds(pl.multiple_of(f2 * 128 + blk * 8, 8), 8)
-            taps = [w_b[t, frows, :] for t in range(TAPS)]
-            moved = []
-            for part in range(2):
-                own = y_v[f2, part, rows, :]
-                edge = pltpu.roll(halos[f2 // 16][part], (N - 8 * (f2 % 16) - 4) % N, 1)
-                acc = taps[HALF] * own
-                for t in range(TAPS):
-                    if t != HALF:
-                        wrapped = lane < t - HALF if t > HALF else lane >= N - HALF + t
-                        src = jnp.where(wrapped, edge, own)
-                        acc = acc + taps[t] * pltpu.roll(src, (HALF - t) % N, 1)
-                moved.append(acc)
-            a_re, a_im = azf_v[0, frows, :], azf_v[1, frows, :]
-            vals.append(
-                (moved[0] * a_re - moved[1] * a_im, moved[0] * a_im + moved[1] * a_re)
-            )
-        vals = fft32(vals, 1)
+            rows = slice(8 * blk, 8 * blk + 8)
+            h_c[grp, 0, rows, :] = jnp.where(slot < HALF, lft, pltpu.roll(rgt, 4, 1))
+            h_c[grp, 1, rows, :] = jnp.where(slot < HALF, pltpu.roll(lft, N - 4, 1), rgt)
+
+    place = lax.broadcasted_iota(jnp.int32, (N, N), 1) // 8
+
+    def migrate(f2, c):
+        frows = pl.ds(pl.multiple_of(f2 * 128, 128), 128)
+        own = jnp.concatenate([y_v[f2, 0], y_v[f2, 1]], axis=0)
+        mask = place == f2 % 16
+        edge = [jnp.where(mask, h_c[f2 // 16, part], 0.0) for part in range(2)]
+        edge = jnp.concatenate(edge, axis=0)
+        moved = dot(jnp.concatenate(split(own), axis=1), shift[0])
+        moved = moved + dot(jnp.concatenate(split(edge), axis=1), shift[1])
+        sums = []
+        for part in range(2):
+            rows = slice(part * N, part * N + N)
+            acc = w_b[HALF, frows, :] * own[rows]
+            for i, t in enumerate(t for t in range(TAPS) if t != HALF):
+                acc = acc + w_b[t, frows, :] * moved[rows, i * N : i * N + N]
+            sums.append(acc)
+        a_re, a_im = azf_v[0, frows, :], azf_v[1, frows, :]
+        y_v[f2, 0] = sums[0] * a_re - sums[1] * a_im
+        y_v[f2, 1] = sums[0] * a_im + sums[1] * a_re
+        return c
+
+    lax.fori_loop(0, J, migrate, 0)
+
+    def back_over_pulses(blk, c):
+        rows = pl.ds(pl.multiple_of(blk * 8, 8), 8)
+        vals = fft32([(y_v[f2, 0, rows, :], y_v[f2, 1, rows, :]) for f2 in range(J)], 1)
         for j in range(J):
             a_re, a_im = aztw[j, 0, rows, :], aztw[j, 1, rows, :]
             v_re, v_im = vals[j]
             y_v[j, 0, rows, :] = v_re * a_re + v_im * a_im
             y_v[j, 1, rows, :] = v_im * a_re - v_re * a_im
-        return c
-
-    lax.fori_loop(0, 16, focus, 0)
-
-    def finish(pair, c):
+        pltpu.make_async_copy(y_v.at[:, :, rows], out.at[:, :, rows], out_sem).start()
+        return c
+
+    lax.fori_loop(0, 16, back_over_pulses, 0)
+    pltpu.make_async_copy(y_v, out, out_sem).wait()
+    for n, (first, count) in enumerate(CHUNKS):
+        left_here = s_v.at[pl.ds(first, count), :, pl.ds(0, N - 1)]
+        pltpu.make_async_copy(left_here, left_here, send_sem.at[n]).wait()
+
+
+def finish(vals, mats_h, out, y_v, mats, o_v, in_sem, out_sem):
+    loads = [pltpu.make_async_copy(mats_h.at[pl.ds(2, 2)], mats, in_sem.at[4])]
+    for q in range(4):
+        rows = pl.ds(8 * q, 8)
+        loads.append(pltpu.make_async_copy(vals.at[rows], y_v.at[rows], in_sem.at[q]))
+    for load in loads:
+        load.start()
+    loads[0].wait()
+
+    def one(pair, c):
         data = jnp.concatenate(
             [
                 jnp.concatenate([y_v[2 * pair + i, 0], y_v[2 * pair + i, 1]], axis=0)
@@ -384,7 +410,7 @@
             ],
             axis=1,
         )
-        done = left_mul(mats[2], mats[3], data) * (1.0 / (N * J))
+        done = left_mul(mats[0], mats[1], data) * (1.0 / (N * J))
         for i in range(2):
             for part in range(2):
                 o_v[2 * pair + i, part] = done[part * N : part * N + N, i * N : i * N + N]
@@ -395,21 +421,20 @@
                 ).start()
         return c
 
-    lax.fori_loop(0, J // 2, finish, 0)
+    for q in range(4):
+        loads[q + 1].wait()
+        lax.fori_loop(4 * q, 4 * q + 4, one, 0)
     pltpu.make_async_copy(o_v, o_v, out_sem).wait()
-    for n, (first, count) in enumerate(CHUNKS):
-        left_here = s_v.at[pl.ds(first, count), :, pl.ds(0, N - 1)]
-        pltpu.make_async_copy(left_here, left_here, send_sem.at[n]).wait()
 
 
 def shards(echoes, replica, rcmc_weights, az_filter):
-    mats, twist, aztw = (jnp.asarray(t) for t in constant_tables())
+    mats, twist, aztw, shift = (jnp.asarray(t) for t in constant_tables())
     parts = len(CHUNKS)
     dma = pltpu.SemaphoreType.DMA
-    out = pl.pallas_call(
+    vals = pl.pallas_call(
         body,
-        out_shape=jax.ShapeDtypeStruct((2, N, J, N), F32),
-        in_specs=[pl.BlockSpec(memory_space=pl.ANY)] * 7,
+        out_shape=jax.ShapeDtypeStruct((J, 2, N, N), F32),
+        in_specs=[pl.BlockSpec(memory_space=pl.ANY)] * 8,
         out_specs=pl.BlockSpec(memory_space=pl.ANY),
         scratch_shapes=[
             pltpu.VMEM((2, J, N * N), BF16),
@@ -427,12 +452,13 @@
             pltpu.VMEM((4, 2 * N, 2 * N), BF16),
             pltpu.VMEM((2, N, N), F32),
             pltpu.VMEM((J, 2, N, N), F32),
+            pltpu.VMEM((2, 2 * N, 7 * N), BF16),
             pltpu.VMEM((16, 2, 8, N), F32),
             pltpu.VMEM((16, 2, 8, N), F32),
             pltpu.VMEM((16, 2, 8, N), F32),
             pltpu.VMEM((16, 2, 8, N), F32),
-            pltpu.VMEM((J, 2, N, N), F32),
-            dma((8,)),
+            pltpu.VMEM((2, 2, N, N), F32),
+            dma((9,)),
             dma((parts,)),
             dma((parts,)),
             dma((parts,)),
@@ -444,7 +470,22 @@
             collective_id=0, has_side_effects=True, vmem_limit_bytes=60 * 2**20
         ),
         name="focus",
-    )(echoes, replica, rcmc_weights, az_filter, mats, twist, aztw)
+    )(echoes, replica, rcmc_weights, az_filter, mats, twist, aztw, shift)
+    out = pl.pallas_call(
+        finish,
+        out_shape=jax.ShapeDtypeStruct((2, N, J, N), F32),
+        in_specs=[pl.BlockSpec(memory_space=pl.ANY)] * 2,
+        out_specs=pl.BlockSpec(memory_space=pl.ANY),
+        scratch_shapes=[
+            pltpu.VMEM((J, 2, N, N), F32),
+            pltpu.VMEM((2, 2 * N, 2 * N), BF16),
+            pltpu.VMEM((J, 2, N, N), F32),
+            dma((5,)),
+            dma(()),
+        ],
+        compiler_params=pltpu.CompilerParams(vmem_limit_bytes=48 * 2**20),
+        name="finish",
+    )(vals, mats)
     return out.reshape(2, N * J, N)
 
 

time: 185 us -> 147 us (0.79)
  Pallas kernels: 180 us -> 144 us
  local copies, waits for them, and re-layouts: 4.47 us -> 2.18 us
    pallas_call x1 -> x2, Pallas kernels: 180 us -> 144 us  [the longest x1 139 us: shards(): pl.pallas_call(body, out_shape=jax.ShapeDtypeStruct((J, 2, N, N), F32), i...]
    unnamed x1 -> x4, local copies, waits for them, and re-layouts: 4.47 us -> 2.18 us
where the time goes in v1:
time: 147 us
  Pallas kernels  144 us (98%)
  local copies, waits for them, and re-layouts  2.18 us (1%)
    pallas_call x1, Pallas kernels, shards(): pl.pallas_call(body, out_shape=jax.ShapeDtypeStruct((J, 2, N, N), F32), i...  139 us
    pallas_call x1, Pallas kernels, shards(): pl.pallas_call(finish, out_shape=jax.ShapeDtypeStruct((2, N, J, N), F32),...  5.44 us

profile of v1, /device:TPU:1, one launch (start us, length us, event | category | flops | bytes accessed | tf_op | source)
XLA Modules:
  0.0 146.7 jit_solution(1410700609292526215)
XLA Ops:
  0.0 0.0 copy-start.1
  0.0 139.0 %focus.1.vals = f32[32,2,128,128]{3,2,1,0:T(8,128)} custom-call(bf16[2,32,16384]{2,1,0:T(8,128)(2,1)} %echoes.1, f32[2,2048]{1,0:T(2,128)} %replica.1, f32[8,4096]{1,0:T(8,128)} %weights.1, bf16[2,4096,128]{2,1,0:T(8,128)(2,1)} %az_filter.1, bf16[4,256,256]{2,1,0:T(8,128)(2,1)} %constant.8.clone.mats_h, f32[2,128,128]{2,1,0:T(8,128)} %constant.9.clone.twist_h, ...), custom_call_target="tpu_custom_call" | custom-call | tf_op jit(solution)/shard_map/focus/pallas_call | solution.py:434
  139.0 0.0 copy-done.1
  139.0 0.0 copy-start
  139.0 2.2 %copy-done = f32[32,2,128,128]{3,2,1,0:T(8,128)S(1)} copy-done((f32[32,2,128,128]{3,2,1,0:T(8,128)S(1)}, f32[32,2,128,128]{3,2,1,0:T(8,128)}, u32[]{:S(2)}) %copy-start) | copy-done | bytes 4194328
  141.2 5.4 %finish.1 = f32[2,128,32,128]{3,2,1,0:T(8,128)} custom-call(f32[32,2,128,128]{3,2,1,0:T(8,128)S(1)} %copy-done, bf16[4,256,256]{2,1,0:T(8,128)(2,1)S(1)} %copy-done.1), custom_call_target="tpu_custom_call" | custom-call | tf_op jit(solution)/shard_map/finish/pallas_call | solution.py:474
Async XLA Ops:
  0.0 139.0 %copy-start.1 = (bf16[4,256,256]{2,1,0:T(8,128)(2,1)S(1)}, bf16[4,256,256]{2,1,0:T(8,128)(2,1)}, u32[]{:S(2)}) copy-start(bf16[4,256,256]{2,1,0:T(8,128)(2,1)} %constant.8.clone.mats_h) | copy-start | bytes 1572868
  139.0 2.2 %copy-start = (f32[32,2,128,128]{3,2,1,0:T(8,128)S(1)}, f32[32,2,128,128]{3,2,1,0:T(8,128)}, u32[]{:S(2)}) copy-start(f32[32,2,128,128]{3,2,1,0:T(8,128)} %focus.1.vals) | copy-start | bytes 12582916

commit v2 on v1

--- a/solution.py
+++ b/solution.py
@@ -17,7 +17,7 @@
 HALF = TAPS // 2
 N = 128
 J = 32
-CHUNKS = ((0, 4), (4, 8), (12, 8), (20, 12))
+CHUNKS = ((0, 4), (4, 8), (12, 12), (24, 8))
 
 
 def constant_tables():
@@ -38,10 +38,10 @@
     az = np.stack([np.cos(ang), -np.sin(ang)], axis=1).astype(np.float32)
     az = np.ascontiguousarray(np.broadcast_to(az[..., None], (J, 2, N, N)))
     lanes = np.arange(N)
-    packed = np.where(lanes % 8 < HALF, lanes % 8 - HALF, N + lanes % 8 - HALF)
+    packed = np.where(lanes % 8 < HALF, lanes % 8, N - 8 + lanes % 8)
     want = [lanes[None, :] + t - HALF for t in range(TAPS) if t != HALF]
     own = np.concatenate([lanes[:, None] == w for w in want], axis=1)
-    edge = np.concatenate([packed[:, None] == w for w in want], axis=1)
+    edge = np.pad(packed[:, None] == lanes[None, :], ((0, 0), (0, 6 * N)))
     shift = np.stack([np.tile(own, (2, 1)), np.tile(edge, (2, 1))]).astype(ml_dtypes.bfloat16)
     return mats, twist, az, shift
 
@@ -117,7 +117,7 @@
 def body(
     echoes, replica, weights, az_filter, mats_h, twist_h, aztw_h, shift_h, out,
     e_v, u_v, rep_v, x_v, kern_v, s_v, r_v, y_v, w_t, w_b, azf_v, az_v, mats, twist, aztw, shift,
-    p_r, p_l, h_l, h_r, h_c, in_sem, send_sem, recv_sem, own_sem, halo_send, halo_recv, out_sem,
+    p_r, p_l, h_l, h_r, h_c, w_p, in_sem, send_sem, recv_sem, own_sem, halo_send, halo_recv, out_sem,
 ):
     seg, sh = lax.axis_index("segment"), lax.axis_index("shard")
     x, y, z = sh // 16, seg * 2 + (sh // 8) % 2, sh % 8
@@ -252,7 +252,7 @@
             half = 1
             loads[4].wait()
             unpack(1)
-        lax.fori_loop(start // 2, (first + count) // 2, compress, 0)
+        lax.fori_loop(start // 2, (first + count) // 2, compress, 0, unroll=2 if n == 0 else 1)
         if n == 0:
             pl.semaphore_wait(barrier, N - 1)
         send(n)
@@ -267,6 +267,18 @@
         return c
 
     lax.fori_loop(0, J, spread, 0)
+    place = lax.broadcasted_iota(jnp.int32, (N, N), 1) // 8
+    slots = lax.broadcasted_iota(jnp.int32, (N, N), 1) % 8
+
+    def pack(i, c):
+        acc = jnp.zeros((N, N), F32)
+        for g in range(16):
+            rows = pl.ds(pl.multiple_of((i % 2) * (16 * N) + g * N, N), N)
+            acc = jnp.where(place == g, w_b[i // 2, rows, :], acc)
+        w_p[i] = acc
+        return c
+
+    lax.fori_loop(0, 2 * TAPS, pack, 0)
     loads[6].wait()
 
     def widen(g, c):
@@ -300,7 +312,7 @@
         pltpu.make_async_copy(s_v.at[rows, :, me], r_v.at[rows, :, me], own_sem.at[n]).wait()
         landed = r_v.at[rows, :, pl.ds(0, N - 1)]
         pltpu.make_async_copy(landed, landed, recv_sem.at[n]).wait()
-        lax.fori_loop(first // 2, (first + count) // 2, over_devices, 0)
+        lax.fori_loop(first // 2, (first + count) // 2, over_devices, 0, unroll=2)
 
     lane = lax.broadcasted_iota(jnp.int32, (8, N), 1)
     slot = lane % 8
@@ -337,6 +349,20 @@
     )
     to_right.start()
     to_left.start()
+
+    def gather(f2, c):
+        frows = pl.ds(pl.multiple_of(f2 * 128, 128), 128)
+        own = jnp.concatenate([y_v[f2, 0], y_v[f2, 1]], axis=0)
+        moved = dot(jnp.concatenate(split(own), axis=1), shift[0])
+        for part in range(2):
+            rows = slice(part * N, part * N + N)
+            acc = w_b[HALF, frows, :] * own[rows]
+            for i, t in enumerate(t for t in range(TAPS) if t != HALF):
+                acc = acc + w_b[t, frows, :] * moved[rows, i * N : i * N + N]
+            y_v[f2, part] = acc
+        return c
+
+    lax.fori_loop(0, J, gather, 0, unroll=2)
     to_right.wait()
     to_left.wait()
 
@@ -351,29 +377,30 @@
             h_c[grp, 0, rows, :] = jnp.where(slot < HALF, lft, pltpu.roll(rgt, 4, 1))
             h_c[grp, 1, rows, :] = jnp.where(slot < HALF, pltpu.roll(lft, N - 4, 1), rgt)
 
-    place = lax.broadcasted_iota(jnp.int32, (N, N), 1) // 8
+    for grp in range(2):
+        for part in range(2):
+            held = h_c[grp, part]
+            acc = jnp.where(slots < HALF, w_p[grp] * held, 0.0)
+            for t in range(1, TAPS):
+                if t != HALF:
+                    moved = pltpu.roll(held, N - t if t < HALF else TAPS - t, 1)
+                    used = slots < HALF - t if t < HALF else slots >= TAPS + HALF - t
+                    acc = acc + jnp.where(used, w_p[2 * t + grp] * moved, 0.0)
+            h_c[grp, part] = acc
 
     def migrate(f2, c):
         frows = pl.ds(pl.multiple_of(f2 * 128, 128), 128)
-        own = jnp.concatenate([y_v[f2, 0], y_v[f2, 1]], axis=0)
         mask = place == f2 % 16
         edge = [jnp.where(mask, h_c[f2 // 16, part], 0.0) for part in range(2)]
         edge = jnp.concatenate(edge, axis=0)
-        moved = dot(jnp.concatenate(split(own), axis=1), shift[0])
-        moved = moved + dot(jnp.concatenate(split(edge), axis=1), shift[1])
-        sums = []
-        for part in range(2):
-            rows = slice(part * N, part * N + N)
-            acc = w_b[HALF, frows, :] * own[rows]
-            for i, t in enumerate(t for t in range(TAPS) if t != HALF):
-                acc = acc + w_b[t, frows, :] * moved[rows, i * N : i * N + N]
-            sums.append(acc)
+        moved = dot(jnp.concatenate(split(edge), axis=1), shift[1, :, :N])
+        sums = [y_v[f2, part] + moved[part * N : part * N + N] for part in range(2)]
         a_re, a_im = azf_v[0, frows, :], azf_v[1, frows, :]
         y_v[f2, 0] = sums[0] * a_re - sums[1] * a_im
         y_v[f2, 1] = sums[0] * a_im + sums[1] * a_re
         return c
 
-    lax.fori_loop(0, J, migrate, 0)
+    lax.fori_loop(0, J, migrate, 0, unroll=4)
 
     def back_over_pulses(blk, c):
         rows = pl.ds(pl.multiple_of(blk * 8, 8), 8)
@@ -423,7 +450,7 @@
 
     for q in range(4):
         loads[q + 1].wait()
-        lax.fori_loop(4 * q, 4 * q + 4, one, 0)
+        lax.fori_loop(4 * q, 4 * q + 4, one, 0, unroll=2)
     pltpu.make_async_copy(o_v, o_v, out_sem).wait()
 
 
@@ -458,6 +485,7 @@
             pltpu.VMEM((16, 2, 8, N), F32),
             pltpu.VMEM((16, 2, 8, N), F32),
             pltpu.VMEM((2, 2, N, N), F32),
+            pltpu.VMEM((2 * TAPS, N, N), F32),
             dma((9,)),
             dma((parts,)),
             dma((parts,)),
@@ -483,7 +511,7 @@
             dma((5,)),
             dma(()),
         ],
-        compiler_params=pltpu.CompilerParams(vmem_limit_bytes=48 * 2**20),
+        compiler_params=pltpu.CompilerParams(vmem_limit_bytes=60 * 2**20),
         name="finish",
     )(vals, mats)
     return out.reshape(2, N * J, N)

time: 147 us -> 132 us (0.90)
  Pallas kernels: 144 us -> 132 us
  local copies, waits for them, and re-layouts: 2.18 us -> 0 us
    pallas_call x1, Pallas kernels: 139 us -> 127 us  [shards(): pl.pallas_call(body, out_shape=jax.ShapeDtypeStruct((J, 2, N, N), F32), i...]
    unnamed x4 -> x0, local copies, waits for them, and re-layouts: 2.18 us -> none
where the time goes in v2:
time: 132 us
  Pallas kernels  132 us (100%)
    pallas_call x1, Pallas kernels, shards(): pl.pallas_call(body, out_shape=jax.ShapeDtypeStruct((J, 2, N, N), F32), i...  127 us
    pallas_call x1, Pallas kernels, shards(): pl.pallas_call(finish, out_shape=jax.ShapeDtypeStruct((2, N, J, N), F32),...  5.36 us

profile of v2, /device:TPU:1, one launch (start us, length us, event | category | flops | bytes accessed | tf_op | source)
XLA Modules:
  0.0 132.0 jit_solution(8594953741110592927)
XLA Ops:
  0.0 126.7 %focus.1.vals = f32[32,2,128,128]{3,2,1,0:T(8,128)} custom-call(bf16[2,32,16384]{2,1,0:T(8,128)(2,1)} %echoes.1, f32[2,2048]{1,0:T(2,128)} %replica.1, f32[8,4096]{1,0:T(8,128)} %weights.1, bf16[2,4096,128]{2,1,0:T(8,128)(2,1)} %az_filter.1, bf16[4,256,256]{2,1,0:T(8,128)(2,1)} %constant.8.clone.mats_h, f32[2,128,128]{2,1,0:T(8,128)} %constant.9.clone.twist_h, ...), custom_call_target="tpu_custom_call" | custom-call | tf_op jit(solution)/shard_map/focus/pallas_call | solution.py:461
  126.7 5.4 %finish.1 = f32[2,128,32,128]{3,2,1,0:T(8,128)} custom-call(f32[32,2,128,128]{3,2,1,0:T(8,128)} %focus.1.vals, bf16[4,256,256]{2,1,0:T(8,128)(2,1)} %constant.8.clone.mats_h), custom_call_target="tpu_custom_call" | custom-call | tf_op jit(solution)/shard_map/finish/pallas_call | solution.py:502
